TPU v7x, 512 devices: a whole 4x8x8 slice. The times are simulated.
512 devices in a mesh: grp: 16 (over y, core), shard: 32 (over x, z).
Axes of the slice: x: 4, y: 8, z: 8, core: 2. Of those that a mesh axis runs over, the one named last changes fastest.
Arguments:
- table: float32 [32768, 64], P('shard'), may hold values from -6 to 6
- accum: float32 [32768, 64], P('shard'), may hold values from 0.1 to 10
- grad_values: float32 [65536, 64], P(('grp', 'shard')), may hold values from -6 to 6
- grad_rows: int32 [65536], P(('grp', 'shard')), may hold values from 0 to 1023
- grad_counts: int32 [16384], P(('grp', 'shard')), may hold values from 1 to 4
- bucket_ids: int32 [131072, 24, 2], P(('grp', 'shard')), may hold values from 0 to 32767, as said below
- bag_lengths: int32 [131072, 24], P(('grp', 'shard')), may hold values from 1 to 2
- w_hidden: bfloat16 [1536, 1024], P('shard'), may hold values from -0.15625 to 0.15625
- b_hidden: float32 [1024], replicated, may hold values from -3 to 3
- w_score: bfloat16 [1024], replicated, may hold values from -0.1875 to 0.1875
Outputs:
- table_out: float32 [32768, 64], P('shard')
- accum_out: float32 [32768, 64], P('shard')
- scores: float32 [131072], P(('grp', 'shard'))
Inputs may be any that keep to these rules, and one draw needn't show every extreme that they name: `bucket_ids`: counting all 24 x 2 id slots of a device's 256 requests, also those past a bag's length, and calling id // 1024 the owner: one owner gets exactly 768 of them, the same owner for every device of one group along grp, and every other owner's count differs from the others' by at most one.
All inputs are finite; a program needn't handle non-finite values.
Results may differ from a plain program's by a relative error of at most 0.0054.
Values may be sent and summed in bfloat16 or wider, within the bound.
No kernel may reach another device: no remote copies, remote signals or barrier semaphores. Data moves between devices by JAX's collectives and lax.ppermute only.
A program may use at most 64 MiB of HBM per device.

v0:
```python
import math
import jax
import jax.numpy as jnp
from jax import lax
from jax.sharding import PartitionSpec as P


def sum_into_rows(row_count, target_rows, slot_values):
    picks = (jnp.arange(row_count, dtype=jnp.int32)[:, None] == target_rows[None, :]).astype(
        jnp.float32
    )
    return jnp.dot(
        picks, slot_values, precision=lax.Precision.HIGHEST, preferred_element_type=jnp.float32
    )


def build_requests(owner_pick, within, local_rows, capacity):
    owner_total = owner_pick.shape[1]
    within_pick = (within[:, None] == jnp.arange(capacity, dtype=jnp.int32)[None, :]).astype(
        jnp.bfloat16
    )
    low_part = (local_rows % 256).astype(jnp.float32)
    high_part = (local_rows // 256).astype(jnp.float32)
    left_side = jnp.concatenate(
        [owner_pick * low_part[:, None], owner_pick * high_part[:, None]], axis=1
    ).astype(jnp.bfloat16)
    packed = jnp.einsum("sk,sc->kc", left_side, within_pick, preferred_element_type=jnp.float32)
    return (packed[owner_total:] * 256.0 + packed[:owner_total]).astype(jnp.int32)


def per_device(
    table,
    accum,
    grad_values,
    grad_rows,
    grad_counts,
    bucket_ids,
    bag_lengths,
    w_hidden,
    b_hidden,
    w_score,
):
    shard_count = lax.axis_size("shard")
    rows_here, row_width = table.shape
    slot_rows = grad_rows.shape[0] // shard_count
    live_rows = jnp.arange(slot_rows, dtype=jnp.int32)[None, :] < grad_counts[:, None]
    grad_slots = jnp.where(
        live_rows[:, :, None], grad_values.reshape(shard_count, slot_rows, row_width), 0.0
    )
    targets = grad_rows.reshape(shard_count, slot_rows)
    got_values, got_rows = (
        lax.all_to_all(grad_slots, "shard", split_axis=0, concat_axis=0, tiled=True),
        lax.all_to_all(targets, "shard", split_axis=0, concat_axis=0, tiled=True),
    )
    owned_sum = sum_into_rows(rows_here, got_rows.reshape(-1), got_values.reshape(-1, row_width))
    grad_sum = lax.psum(owned_sum, "grp")
    accum_out = accum + grad_sum * grad_sum
    table_out = table - 0.5 * grad_sum * lax.rsqrt(accum_out)
    serving_rows = table_out.astype(jnp.bfloat16)
    request_count, vocab_count, bag_size = bucket_ids.shape
    flat_ids = bucket_ids.reshape(-1)
    slot_count = flat_ids.shape[0]
    capacity = 2 * slot_count // shard_count
    owners = flat_ids // rows_here
    local_rows = flat_ids % rows_here
    owner_iota = jnp.arange(shard_count, dtype=jnp.int32)
    block_len = math.gcd(slot_count, 256)
    block_total = slot_count // block_len
    owner_hot = (
        owners.reshape(block_total, block_len)[:, :, None] == owner_iota[None, None, :]
    ).astype(jnp.bfloat16)
    position = jnp.arange(block_len, dtype=jnp.int32)
    lower_ones = (position[:, None] >= position[None, :]).astype(jnp.bfloat16)
    inclusive = jnp.einsum("ij,bjk->bik", lower_ones, owner_hot, preferred_element_type=jnp.float32)
    owner_float = owner_hot.astype(jnp.float32)
    block_sums = jnp.sum(owner_float, axis=1)
    block_offsets = jnp.cumsum(block_sums, axis=0) - block_sums
    ranks = inclusive + block_offsets[:, None, :]
    within = (jnp.sum(owner_float * ranks, axis=2) - 1.0).reshape(-1).astype(jnp.int32)
    owner_pick = owner_float.reshape(slot_count, shard_count)
    placed = owners * capacity + within
    requested = build_requests(owner_pick, within, local_rows, capacity)
    fetched = serving_rows[
        lax.all_to_all(requested, "shard", split_axis=0, concat_axis=0, tiled=True)
    ]
    returned = lax.all_to_all(fetched, "shard", split_axis=0, concat_axis=0, tiled=True)
    own_rows = returned.reshape(shard_count * capacity, row_width)[placed]
    own_rows = own_rows.reshape(request_count, vocab_count, bag_size, row_width)
    in_bag = jnp.arange(bag_size, dtype=jnp.int32)[None, None, :] < bag_lengths[:, :, None]
    pooled = jnp.sum(jnp.where(in_bag[..., None], own_rows.astype(jnp.float32), 0.0), axis=2)
    pooled = pooled.astype(jnp.bfloat16).reshape(request_count, vocab_count * row_width)
    hidden_pre = jnp.dot(
        pooled,
        lax.all_gather(w_hidden, "shard", axis=0, tiled=True),
        preferred_element_type=jnp.float32,
    )
    hidden = jax.nn.silu(hidden_pre + b_hidden).astype(jnp.bfloat16)
    scores = jnp.dot(hidden, w_score, preferred_element_type=jnp.float32)
    return (table_out, accum_out, scores)


def solution(mesh):
    return jax.shard_map(
        per_device,
        mesh=mesh,
        in_specs=(
            P("shard", None),
            P("shard", None),
            P(("grp", "shard"), None),
            P(("grp", "shard")),
            P(("grp", "shard")),
            P(("grp", "shard"), None, None),
            P(("grp", "shard"), None),
            P("shard", None),
            P(),
            P(),
        ),
        out_specs=(P("shard", None), P("shard", None), P(("grp", "shard"))),
        check_vma=False,
    )
```

profile of v0, /device:TPU:6, one launch (start us, length us, event | category | flops | bytes accessed | tf_op | source)
XLA Modules:
  0.0 444.5 jit_solution(10169167343859944870)
XLA Ops:
  8.0 1.4 all_to_all.20
  9.4 13.4 %all-to-all-start = ((s32[32,1,4]{2,1,0:T(1,128)}), s32[32,1,4]{2,1,0:T(1,128)S(1)}, u32[]{:S(2)}, u32[]{:S(2)}) async-start(s32[32,1,4]{2,1,0:T(1,128)} %bitcast), calls=%async_computation | async-start | bytes 32768 | tf_op jit(solution)/shard_map/all_to_all | solution.py:53
  22.8 1.8 copy.46
  24.7 2.1 reshape.301
  26.8 2.1 reshape.302
  31.2 7.7 %fusion = f32[64,768]{1,0:T(8,128)S(1)} fusion(s32[12288]{0:T(1024)S(1)} %bitcast.41, bf16[12288,32]{0,1:T(8,128)(2,1)S(1)} %get-tuple-element.9, bf16[12288,32]{0,1:T(8,128)(2,1)S(1)} %get-tuple-element.8), kind=kOutput, calls=%fused_computation.3 | convolution fusion | flops 1220542464 | bytes 1818624 | tf_op jit(solution)/shard_map/sk,sc->kc/dot_general | solution.py:27
  39.7 9.8 %all-to-all-start.1 = ((f32[32,1,256]{2,1,0:T(1,128)}), f32[32,1,256]{2,1,0:T(1,128)S(1)}, u32[]{:S(2)}, u32[]{:S(2)}) async-start(f32[32,1,256]{2,1,0:T(1,128)} %reshape.335), calls=%async_computation.1 | async-start | bytes 65536 | tf_op jit(solution)/shard_map/all_to_all | solution.py:52
  51.6 6.0 %all-to-all-done.1 = f32[32,1,256]{2,1,0:T(1,128)S(1)} async-done(((f32[32,1,256]{2,1,0:T(1,128)}), f32[32,1,256]{2,1,0:T(1,128)S(1)}, u32[]{:S(2)}, u32[]{:S(2)}) %all-to-all-start.1) | async-done | bytes 32800 | tf_op jit(solution)/shard_map/all_to_all | solution.py:52
  57.5 5.7 %all-to-all-start.2 = ((s32[32,1,768]{2,1,0:T(1,128)}), s32[32,1,768]{2,1,0:T(1,128)S(1)}, u32[]{:S(2)}, u32[]{:S(2)}) async-start(s32[32,1,768]{2,1,0:T(1,128)} %copy.48), calls=%async_computation.2 | async-start | bytes 196608 | tf_op jit(solution)/shard_map/all_to_all | solution.py:84
  64.7 1.1 fusion.16
  65.8 5.8 %all-to-all-done.2 = s32[32,1,768]{2,1,0:T(1,128)S(1)} async-done(((s32[32,1,768]{2,1,0:T(1,128)}), s32[32,1,768]{2,1,0:T(1,128)S(1)}, u32[]{:S(2)}, u32[]{:S(2)}) %all-to-all-start.2) | async-done | bytes 98336 | tf_op jit(solution)/shard_map/all_to_all | solution.py:84
  72.3 109.3 %all-reduce.2.cloned.1.call-done = f32[1024,64]{0,1:T(8,128)} async-done(((f32[1024,64]{0,1:T(8,128)}), f32[1024,64]{0,1:T(8,128)}) %all-reduce.2.cloned.1.call-update) | async-done | bytes 262160 | tf_op jit(solution)/shard_map/psum | solution.py:56
  181.7 2.0 fusion.32
  183.8 93.6 %gather_fusion = bf16[24576,64]{1,0:T(8,128)(2,1)} fusion(bf16[1024,64]{1,0:T(8,128)(2,1)S(1)} %copy.49, s32[24576]{0:T(1024)} %broadcast_clamp_fusion), kind=kCustom, calls=%fused_computation | custom fusion | bytes 6389760 | tf_op jit(solution)/shard_map/gather | solution.py:83
  277.4 6.8 %copy.50 = bf16[32,768,64]{1,2,0:T(8,128)(2,1)} copy(bf16[32,768,64]{2,1,0:T(8,128)(2,1)} %bitcast.33) | data formatting | bytes 6291456 | tf_op jit(solution)/shard_map/gather | solution.py:83
  284.3 10.6 %all-to-all-start.3 = ((bf16[32,768,64]{1,2,0:T(8,128)(2,1)}), bf16[32,768,64]{1,2,0:T(8,128)(2,1)}, u32[]{:S(2)}, u32[]{:S(2)}) async-start(bf16[32,768,64]{1,2,0:T(8,128)(2,1)} %copy.50), calls=%async_computation.3 | async-start | bytes 6291456 | tf_op jit(solution)/shard_map/all_to_all | solution.py:86
  295.5 2.2 reshape.304
  297.9 2.2 iota_compare_fusion.2
  300.4 72.3 %all-to-all-done.3 = bf16[32,768,64]{1,2,0:T(8,128)(2,1)} async-done(((bf16[32,768,64]{1,2,0:T(8,128)(2,1)}), bf16[32,768,64]{1,2,0:T(8,128)(2,1)}, u32[]{:S(2)}, u32[]{:S(2)}) %all-to-all-start.3) | async-done | bytes 3145760 | tf_op jit(solution)/shard_map/all_to_all | solution.py:86
  372.7 6.6 %copy.51 = bf16[32,768,64]{2,1,0:T(8,128)(2,1)} copy(bf16[32,768,64]{1,2,0:T(8,128)(2,1)} %all-to-all-done.3) | data formatting | bytes 6291456 | tf_op jit(solution)/shard_map/all_to_all | solution.py:86
  379.3 36.4 %gather_fusion.1 = bf16[12288,64]{1,0:T(8,128)(2,1)S(1)} fusion(bf16[24576,64]{1,0:T(8,128)(2,1)} %bitcast.32, s32[12288]{0:T(1024)S(1)} %broadcast_clamp_fusion.1), kind=kCustom, calls=%fused_computation.1 | custom fusion | bytes 3194880 | tf_op jit(solution)/shard_map/gather | solution.py:87
  415.8 15.5 %fusion.2 = bf16[256,24,64]{2,1,0:T(8,128)(2,1)} fusion(bf16[256,24,2,64]{3,2,1,0:T(2,128)(2,1)S(1)} %bitcast.34, pred[256,24,2]{2,1,0:T(8,128)(4,1)} %iota_compare_fusion.2), kind=kLoop, calls=%fused_computation.6 | loop fusion | flops 1966080 | bytes 2371584 | tf_op jit(solution)/shard_map/reduce_sum | solution.py:90
  431.3 2.0 copy.53
  433.3 3.7 fusion.12
  (47 shorter events, 8.5 us)
Async XLA Ops:
  9.4 30.3 %all-to-all-start = ((s32[32,1,4]{2,1,0:T(1,128)}), s32[32,1,4]{2,1,0:T(1,128)S(1)}, u32[]{:S(2)}, u32[]{:S(2)}) async-start(s32[32,1,4]{2,1,0:T(1,128)} %bitcast), calls=%async_computation | async-start | bytes 32768 | tf_op jit(solution)/shard_map/all_to_all | solution.py:53
  26.8 4.0 copy-start.1
  26.8 4.1 copy-start.4
  39.7 17.8 %all-to-all-start.1 = ((f32[32,1,256]{2,1,0:T(1,128)}), f32[32,1,256]{2,1,0:T(1,128)S(1)}, u32[]{:S(2)}, u32[]{:S(2)}) async-start(f32[32,1,256]{2,1,0:T(1,128)} %reshape.335), calls=%async_computation.1 | async-start | bytes 65536 | tf_op jit(solution)/shard_map/all_to_all | solution.py:52
  57.5 14.1 %all-to-all-start.2 = ((s32[32,1,768]{2,1,0:T(1,128)}), s32[32,1,768]{2,1,0:T(1,128)S(1)}, u32[]{:S(2)}, u32[]{:S(2)}) async-start(s32[32,1,768]{2,1,0:T(1,128)} %copy.48), calls=%async_computation.2 | async-start | bytes 196608 | tf_op jit(solution)/shard_map/all_to_all | solution.py:84
  63.3 118.4 %all-reduce.2.cloned.1.call-start = ((), (), s32[]{:S(2)}) async-start(), calls=%async_computation.4 | async-start | bytes 524288 | tf_op jit(solution)/shard_map/psum | solution.py:56
  284.3 88.4 %all-to-all-start.3 = ((bf16[32,768,64]{1,2,0:T(8,128)(2,1)}), bf16[32,768,64]{1,2,0:T(8,128)(2,1)}, u32[]{:S(2)}, u32[]{:S(2)}) async-start(bf16[32,768,64]{1,2,0:T(8,128)(2,1)} %copy.50), calls=%async_computation.3 | async-start | bytes 6291456 | tf_op jit(solution)/shard_map/all_to_all | solution.py:86
  294.9 2.8 copy-start
  294.9 2.9 copy-start.2
  294.9 3.0 copy-start.3
  294.9 138.4 %all-gather.2.cloned.1.call-start = ((), (), s32[]{:S(2)}) async-start(), calls=%async_computation.5 | async-start | bytes 3244032 | tf_op jit(solution)/shard_map/all_gather | solution.py:94
  415.8 17.6 %copy-start.5 = (f32[1024]{0:T(1024)S(1)}, f32[1024]{0:T(1024)}, u32[]{:S(2)}) copy-start(f32[1024]{0:T(1024)} %param.18) | copy-start | bytes 12292
Sparse Core Ops, SparseCore 0:
  67.0 114.6 all-reduce.1
Sparse Core Ops, SparseCore 1:
  299.0 94.9 all-gather.1
where the time goes:
time: 447 us; the launch traced here: 445 us
  waiting for transfers between devices  194 us (43%)
  local copies, waits for them, and re-layouts  158 us (35%)
  starting transfers between devices  39.6 us (9%)
  other arithmetic  23.7 us (5%)
  between operations  15.8 us (4%)
  matrix products  13.2 us (3%)
    psum x1, waiting for transfers between devices, per_device(): grad_sum = lax.psum(owned_sum, 'grp')  109 us
    gather x2, local copies, waits for them, and re-layouts, per_device(): serving_rows[lax.all_to_all(requested, 'shard', split_axis=0, concat_axis...  100 us
    all_to_all x1, waiting for transfers between devices, per_device(): lax.all_to_all(fetched, 'shard', split_axis=0, concat_axis=0, tiled=True)  72.3 us
    gather x1, local copies, waits for them, and re-layouts, per_device(): own_rows = returned.reshape(shard_count * capacity, row_width)[placed]  36.4 us
    reduce_sum x1, other arithmetic, per_device(): jnp.sum(jnp.where(in_bag[..., None], own_rows.astype(jnp.float32), 0.0),...  15.5 us
    all_to_all x1, starting transfers between devices, per_device(): lax.all_to_all(targets, 'shard', split_axis=0, concat_axis=0, tiled=True)  13.4 us
    all_to_all x1, starting transfers between devices, per_device(): lax.all_to_all(fetched, 'shard', split_axis=0, concat_axis=0, tiled=True)  10.6 us
    all_to_all x1, starting transfers between devices, per_device(): lax.all_to_all(grad_slots, 'shard', split_axis=0, concat_axis=0, tiled=True)  9.78 us
  transfers between devices with their start and end apart: 6, of which 4 were waited for; matrix products, arithmetic and copies ran while one was open for 20% of the time, Pallas kernels for 0%

commit v1 on v0

--- a/solution.py
+++ b/solution.py
@@ -53,7 +53,7 @@
         lax.all_to_all(targets, "shard", split_axis=0, concat_axis=0, tiled=True),
     )
     owned_sum = sum_into_rows(rows_here, got_rows.reshape(-1), got_values.reshape(-1, row_width))
-    grad_sum = lax.psum(owned_sum, "grp")
+    grad_sum = jnp.sum(lax.all_gather(owned_sum, "grp"), axis=0)
     accum_out = accum + grad_sum * grad_sum
     table_out = table - 0.5 * grad_sum * lax.rsqrt(accum_out)
     serving_rows = table_out.astype(jnp.bfloat16)

time: 447 us -> 361 us (0.81)
  waiting for transfers between devices: 194 us -> 96.5 us
  blocking collectives: 0 us -> 13.2 us
  starting transfers between devices: 39.6 us -> 29.5 us
  local copies, waits for them, and re-layouts: 158 us -> 163 us
    psum x1 -> x0, waiting for transfers between devices: 109 us -> none  [per_device(): grad_sum = lax.psum(owned_sum, 'grp')]
    all_to_all x0 -> x1, blocking collectives: none -> 13.2 us  [per_device(): lax.all_to_all(requested, 'shard', split_axis=0, concat_axis=0, tiled=True)]
    all_gather x0 -> x1, waiting for transfers between devices: none -> 11.2 us  [per_device(): grad_sum = jnp.sum(lax.all_gather(owned_sum, 'grp'), axis=0)]
    all_to_all x1 -> x0, waiting for transfers between devices: 5.77 us -> none  [per_device(): lax.all_to_all(requested, 'shard', split_axis=0, concat_axis=0, tiled=True)]
    all_to_all x1 -> x0, starting transfers between devices: 5.74 us -> none  [per_device(): lax.all_to_all(requested, 'shard', split_axis=0, concat_axis=0, tiled=True)]
    unnamed x20 -> x21, local copies, waits for them, and re-layouts: 2.96 us -> 8.64 us
    all_to_all x1, waiting for transfers between devices: 0.01 us -> 5.41 us  [per_device(): lax.all_to_all(targets, 'shard', split_axis=0, concat_axis=0, tiled=True)]
  transfers between devices with their start and end apart: 6 -> 5, of which waited for: 4 -> 4; matrix products, arithmetic and copies ran while one was open for 20% -> 24% of each run, Pallas kernels for 0% -> 0%
where the time goes in v1:
time: 361 us; the launch traced here: 356 us
  local copies, waits for them, and re-layouts  163 us (45%)
  waiting for transfers between devices  96.5 us (27%)
  starting transfers between devices  29.5 us (8%)
  other arithmetic  24.4 us (7%)
  between operations  15.8 us (4%)
  matrix products  13.2 us (4%)
  blocking collectives  13.2 us (4%)
    gather x2, local copies, waits for them, and re-layouts, per_device(): serving_rows[lax.all_to_all(requested, 'shard', split_axis=0, concat_axis...  100 us
    all_to_all x1, waiting for transfers between devices, per_device(): lax.all_to_all(fetched, 'shard', split_axis=0, concat_axis=0, tiled=True)  72.8 us
    gather x1, local copies, waits for them, and re-layouts, per_device(): own_rows = returned.reshape(shard_count * capacity, row_width)[placed]  36.4 us
    reduce_sum x1, other arithmetic, per_device(): jnp.sum(jnp.where(in_bag[..., None], own_rows.astype(jnp.float32), 0.0),...  15.5 us
    all_to_all x1, starting transfers between devices, per_device(): lax.all_to_all(targets, 'shard', split_axis=0, concat_axis=0, tiled=True)  13.4 us
    all_to_all x1, blocking collectives, per_device(): lax.all_to_all(requested, 'shard', split_axis=0, concat_axis=0, tiled=True)  13.2 us
    all_gather x1, waiting for transfers between devices, per_device(): grad_sum = jnp.sum(lax.all_gather(owned_sum, 'grp'), axis=0)  11.2 us
    all_to_all x1, starting transfers between devices, per_device(): lax.all_to_all(fetched, 'shard', split_axis=0, concat_axis=0, tiled=True)  10.2 us
  transfers between devices with their start and end apart: 5, of which 4 were waited for; matrix products, arithmetic and copies ran while one was open for 24% of the time, Pallas kernels for 0%

profile of v1, /device:TPU:6, one launch (start us, length us, event | category | flops | bytes accessed | tf_op | source)
XLA Modules:
  0.0 355.8 jit_solution(15437100690890184723)
XLA Ops:
  8.0 1.4 all_to_all.20
  9.4 13.4 %all-to-all-start = ((s32[32,1,4]{2,1,0:T(1,128)}), s32[32,1,4]{2,1,0:T(1,128)S(1)}, u32[]{:S(2)}, u32[]{:S(2)}) async-start(s32[32,1,4]{2,1,0:T(1,128)} %bitcast), calls=%async_computation | async-start | bytes 32768 | tf_op jit(solution)/shard_map/all_to_all | solution.py:53
  25.2 5.4 %all-to-all-done = s32[32,1,4]{2,1,0:T(1,128)S(1)} async-done(((s32[32,1,4]{2,1,0:T(1,128)}), s32[32,1,4]{2,1,0:T(1,128)S(1)}, u32[]{:S(2)}, u32[]{:S(2)}) %all-to-all-start) | async-done | bytes 544 | tf_op jit(solution)/shard_map/all_to_all | solution.py:53
  30.7 5.7 %all-to-all-start.1 = ((f32[32,1,256]{2,1,0:T(1,128)}), f32[32,1,256]{2,1,0:T(1,128)S(1)}, u32[]{:S(2)}, u32[]{:S(2)}) async-start(f32[32,1,256]{2,1,0:T(1,128)} %reshape.336), calls=%async_computation.1 | async-start | bytes 65536 | tf_op jit(solution)/shard_map/all_to_all | solution.py:52
  37.8 6.6 %all-to-all-done.1 = f32[32,1,256]{2,1,0:T(1,128)S(1)} async-done(((f32[32,1,256]{2,1,0:T(1,128)}), f32[32,1,256]{2,1,0:T(1,128)S(1)}, u32[]{:S(2)}, u32[]{:S(2)}) %all-to-all-start.1) | async-done | bytes 32800 | tf_op jit(solution)/shard_map/all_to_all | solution.py:52
  45.6 1.1 fusion.16
  46.8 2.0 copy.64
  48.8 2.1 reshape.301
  50.9 2.1 reshape.302
  55.2 7.7 %fusion = f32[64,768]{1,0:T(8,128)S(1)} fusion(s32[12288]{0:T(1024)S(1)} %bitcast.47, bf16[12288,32]{0,1:T(8,128)(2,1)S(1)} %get-tuple-element.21, bf16[12288,32]{0,1:T(8,128)(2,1)S(1)} %get-tuple-element.20), kind=kOutput, calls=%fused_computation.3 | convolution fusion | flops 1220542464 | bytes 1818624 | tf_op jit(solution)/shard_map/sk,sc->kc/dot_general | solution.py:27
  63.0 13.2 %all_to_all.31 = s32[32,1,768]{2,1,0:T(1,128)S(1)} all-to-all(s32[32,1,768]{2,1,0:T(1,128)S(1)} %copy.66), channel_id=1, replica_groups=mesh['grp'=16,'shard'=32] {'shard'}, dimensions={0} | all-to-all | bytes 196608 | tf_op jit(solution)/shard_map/all_to_all | solution.py:84
  76.9 11.2 %all-gather.6.cloned.1.call-done = f32[16384,64]{0,1:T(8,128)} async-done(((f32[1024,64]{0,1:T(8,128)}), f32[16384,64]{0,1:T(8,128)}) %all-gather.6.cloned.1.call-update) | async-done | bytes 4194320 | tf_op jit(solution)/shard_map/all_gather | solution.py:56
  88.1 4.6 %copy.72 = f32[8,8,16,1024]{3,2,1,0:T(8,128)S(1)} copy(f32[8,8,16,1024]{3,1,2,0:T(8,128)} %bitcast.40) | data formatting | bytes 8388608
  94.7 93.7 %gather_fusion = bf16[24576,64]{1,0:T(8,128)(2,1)} fusion(bf16[1024,64]{1,0:T(8,128)(2,1)S(1)} %copy.67, s32[24576]{0:T(1024)} %broadcast_clamp_fusion), kind=kCustom, calls=%fused_computation | custom fusion | bytes 6389760 | tf_op jit(solution)/shard_map/gather | solution.py:83
  188.4 6.8 %copy.68 = bf16[32,768,64]{1,2,0:T(8,128)(2,1)} copy(bf16[32,768,64]{2,1,0:T(8,128)(2,1)} %bitcast.38) | data formatting | bytes 6291456 | tf_op jit(solution)/shard_map/gather | solution.py:83
  195.2 10.2 %all-to-all-start.3 = ((bf16[32,768,64]{1,2,0:T(8,128)(2,1)}), bf16[32,768,64]{1,2,0:T(8,128)(2,1)}, u32[]{:S(2)}, u32[]{:S(2)}) async-start(bf16[32,768,64]{1,2,0:T(8,128)(2,1)} %copy.68), calls=%async_computation.3 | async-start | bytes 6291456 | tf_op jit(solution)/shard_map/all_to_all | solution.py:86
  206.1 2.2 reshape.304
  208.5 2.5 iota_compare_fusion.2
  211.2 72.8 %all-to-all-done.3 = bf16[32,768,64]{1,2,0:T(8,128)(2,1)} async-done(((bf16[32,768,64]{1,2,0:T(8,128)(2,1)}), bf16[32,768,64]{1,2,0:T(8,128)(2,1)}, u32[]{:S(2)}, u32[]{:S(2)}) %all-to-all-start.3) | async-done | bytes 3145760 | tf_op jit(solution)/shard_map/all_to_all | solution.py:86
  284.0 6.6 %copy.69 = bf16[32,768,64]{2,1,0:T(8,128)(2,1)} copy(bf16[32,768,64]{1,2,0:T(8,128)(2,1)} %all-to-all-done.3) | data formatting | bytes 6291456 | tf_op jit(solution)/shard_map/all_to_all | solution.py:86
  290.6 36.4 %gather_fusion.1 = bf16[12288,64]{1,0:T(8,128)(2,1)S(1)} fusion(bf16[24576,64]{1,0:T(8,128)(2,1)} %bitcast.37, s32[12288]{0:T(1024)S(1)} %broadcast_clamp_fusion.1), kind=kCustom, calls=%fused_computation.1 | custom fusion | bytes 3194880 | tf_op jit(solution)/shard_map/gather | solution.py:87
  327.1 15.5 %fusion.2 = bf16[256,24,64]{2,1,0:T(8,128)(2,1)} fusion(bf16[256,24,2,64]{3,2,1,0:T(2,128)(2,1)S(1)} %bitcast.39, pred[256,24,2]{2,1,0:T(8,128)(4,1)} %iota_compare_fusion.2), kind=kLoop, calls=%fused_computation.6 | loop fusion | flops 1966080 | bytes 2371584 | tf_op jit(solution)/shard_map/reduce_sum | solution.py:90
  342.6 2.0 copy.71
  344.6 3.7 %fusion.12 = f32[1,256]{1,0:T(1,128)} fusion(bf16[1024,1]{0,1:T(2,128)(2,1)S(1)} %reshape.325, bf16[256,1536]{0,1:T(8,128)(2,1)S(1)} %bitcast.41, bf16[1536,1024]{1,0:T(8,128)(2,1)} %all-gather.4.cloned.1.call-done, f32[1024]{0:T(1024)S(1)} %copy-done.5), kind=kOutput, calls=%fused_computation.26 | convolution fusion | flops 807403520 | bytes 3939328 | tf_op jit(solution)/shard_map/dot_general | solution.py:98
  (48 shorter events, 11.1 us)
Async XLA Ops:
  9.4 21.3 %all-to-all-start = ((s32[32,1,4]{2,1,0:T(1,128)}), s32[32,1,4]{2,1,0:T(1,128)S(1)}, u32[]{:S(2)}, u32[]{:S(2)}) async-start(s32[32,1,4]{2,1,0:T(1,128)} %bitcast), calls=%async_computation | async-start | bytes 32768 | tf_op jit(solution)/shard_map/all_to_all | solution.py:53
  30.7 13.7 %all-to-all-start.1 = ((f32[32,1,256]{2,1,0:T(1,128)}), f32[32,1,256]{2,1,0:T(1,128)S(1)}, u32[]{:S(2)}, u32[]{:S(2)}) async-start(f32[32,1,256]{2,1,0:T(1,128)} %reshape.336), calls=%async_computation.1 | async-start | bytes 65536 | tf_op jit(solution)/shard_map/all_to_all | solution.py:52
  36.4 51.7 %all-gather.6.cloned.1.call-start = ((), (), s32[]{:S(2)}) async-start(), calls=%async_computation.5 | async-start | bytes 4456448 | tf_op jit(solution)/shard_map/all_gather | solution.py:56
  92.7 1.0 copy-start
  92.7 1.0 copy-start.1
  195.2 88.8 %all-to-all-start.3 = ((bf16[32,768,64]{1,2,0:T(8,128)(2,1)}), bf16[32,768,64]{1,2,0:T(8,128)(2,1)}, u32[]{:S(2)}, u32[]{:S(2)}) async-start(bf16[32,768,64]{1,2,0:T(8,128)(2,1)} %copy.68), calls=%async_computation.3 | async-start | bytes 6291456 | tf_op jit(solution)/shard_map/all_to_all | solution.py:86
  205.4 2.8 copy-start.2
  205.5 2.9 copy-start.3
  205.5 3.0 copy-start.4
  205.5 139.1 %all-gather.4.cloned.1.call-start = ((), (), s32[]{:S(2)}) async-start(), calls=%async_computation.4 | async-start | bytes 3244032 | tf_op jit(solution)/shard_map/all_gather | solution.py:94
  327.1 17.6 %copy-start.5 = (f32[1024]{0:T(1024)S(1)}, f32[1024]{0:T(1024)}, u32[]{:S(2)}) copy-start(f32[1024]{0:T(1024)} %param.18) | copy-start | bytes 12292
Sparse Core Ops, SparseCore 0:
  46.9 41.1 all-gather.5
Sparse Core Ops, SparseCore 1:
  209.1 94.5 all-gather.3
